TPU v7x, 32 devices: a whole 2x2x4 slice. The times are simulated.
32 devices in a mesh: groups: 2 (over y), sector: 4 (over z), op: 4 (over x, core).
Axes of the slice: x: 2, y: 2, z: 4, core: 2. Of those that a mesh axis runs over, the one named last changes fastest.
Arguments:
- left_arrival: bfloat16 [256, 4, 256, 256], P(('groups', 'sector', 'op')), parts along dimension 0, may hold values from -0.1 to 0.15
- right_env: bfloat16 [8, 4, 8, 4, 256, 256], P('groups', 'op', None, 'sector'), parts along dimension 0, may hold values from -0.8 to 1.2
- op_charge: int32 [256], P('groups'), parts along dimension 0, may hold values from -1 to 1
- sector_dims: int32 [8], P(('groups', 'sector')), parts along dimension 0, may hold values from 192 to 256
- wavefunction: bfloat16 [8, 256, 256], P(('groups', 'sector')), parts along dimension 0, may hold values from -300 to 300
- onsite: float32 [8, 256, 256], P(('groups', 'sector')), parts along dimension 0, may hold values from 1 to 6
Outputs:
- last_image: float32 [8, 256, 256], P(('groups', 'sector')), parts along dimension 0
- correlation_matrix: float32 [6, 3], P('groups'), parts along dimension 0
There are 2 independent parts, one for each index of `groups`. A program takes and returns all parts, laid end to end along the dimension named above; each array names one. Nothing has to cross between parts.
All inputs are finite; a program needn't handle non-finite values.
Results may differ from a plain program's by a relative error of at most 0.012.
Values may be sent and summed in bfloat16 or wider, within the bound.
A program may use at most 64 MiB of HBM per device.

v0:
```python
import jax
import jax.numpy as jnp
from jax import lax
from jax.sharding import PartitionSpec as P


def with_halo(block, sides, width):
    for axis, dim in sides:
        count = lax.axis_size(axis)
        forward = [(i, i + 1) for i in range(count - 1)]
        backward = [(target, source) for source, target in forward]
        low = lax.ppermute(
            lax.slice_in_dim(block, block.shape[dim] - width, None, axis=dim), axis, forward
        )
        high = lax.ppermute(lax.slice_in_dim(block, 0, width, axis=dim), axis, backward)
        block = jnp.concatenate([low, block, high], axis=dim)
    return block


def contract(tensor_pieces, operand_state):
    return jnp.einsum(
        "ktab,ktbc->ktac", tensor_pieces, operand_state, preferred_element_type=jnp.float32
    ).astype(jnp.bfloat16)


def on_device(left_arrival, right_env, op_charge, sector_dims, wavefunction, onsite):
    charge_classes_number = lax.axis_size("sector")
    op_count = lax.axis_size("op")
    sec_local = wavefunction.shape[0]
    states = wavefunction.shape[1]
    entries = charge_classes_number * sec_local * states * states
    right_local = right_env.reshape(-1, sec_local, states, states)
    grouped = op_charge.reshape(charge_classes_number, op_count, -1)
    charges = lax.dynamic_slice_in_dim(grouped, lax.axis_index("op"), 1, 1).reshape(-1)
    positions = jnp.arange(states, dtype=jnp.int32)
    inside = positions[None, :] < sector_dims[:, None]
    sector_mask = (inside[:, :, None] & inside[:, None, :]).astype(jnp.float32)

    def total_sums(values):
        return lax.psum(values, "sector")

    def sources(full_vector):
        padded = with_halo(full_vector, (("sector", 0),), 1)
        shifted = jnp.stack([padded[2:], padded[1:-1], padded[:-2]])
        return jnp.take(shifted, charges + 1, axis=0)

    def finish(middle_portion, vector):
        partial_image = jnp.einsum(
            "ktac,ktdc->tad", middle_portion, right_local, preferred_element_type=jnp.float32
        )
        summed = lax.psum(partial_image, "op")
        return sector_mask * (onsite * vector.astype(jnp.float32) + summed)

    masked = sector_mask * wavefunction.astype(jnp.float32)
    start_norm = total_sums((jnp.sum(masked * masked),))[0]
    first_vector = (masked / jnp.sqrt(start_norm / entries + 1e-06)).astype(jnp.bfloat16)
    first_source = sources(first_vector)
    block_rows = lax.all_to_all(left_arrival, "sector", split_axis=1, concat_axis=0, tiled=True)
    first_inner = contract(block_rows, first_source)
    vectors = [first_vector]
    images = [finish(first_inner, first_vector)]
    self_norms = []
    for section in range(2):
        current = vectors[section].astype(jnp.float32)
        image = images[section]
        ritz = total_sums((jnp.sum(current * image), jnp.sum(current * current)))
        self_norms.append(ritz[1])
        rayleigh = ritz[0] / ritz[1]
        correction = (image - rayleigh * current) / (1.0 + jnp.abs(onsite - rayleigh))
        coefficient_images = total_sums(
            tuple(
                (
                    jnp.sum(vectors[earlier].astype(jnp.float32) * correction)
                    for earlier in range(section + 1)
                )
            )
        )
        factors = [
            coefficient_images[earlier] / self_norms[earlier] for earlier in range(section + 1)
        ]
        update = correction
        for earlier in range(section + 1):
            update = update - factors[earlier] * vectors[earlier].astype(jnp.float32)
        length_sq = total_sums((jnp.sum(update * update),))[0]
        vectors.append((update / jnp.sqrt(length_sq / entries + 1e-06)).astype(jnp.bfloat16))
        hamiltonian_vector = vectors[-1]
        images.append(finish(contract(block_rows, sources(hamiltonian_vector)), hamiltonian_vector))
    correlation_values = total_sums(
        tuple(
            (
                jnp.sum(vectors[row].astype(jnp.float32) * images[column])
                for row in range(3)
                for column in range(3)
            )
        )
    )
    correlation_matrix = jnp.stack(correlation_values).reshape(3, 3) / entries
    last_image = images[2]
    return (last_image, correlation_matrix)


def solution(mesh):
    in_specs = (
        P(("groups", "sector", "op"), None, None, None),
        P("groups", "op", None, "sector", None, None),
        P("groups"),
        P(("groups", "sector")),
        P(("groups", "sector"), None, None),
        P(("groups", "sector"), None, None),
    )
    out_specs = (P(("groups", "sector"), None, None), P("groups", None))
    return jax.shard_map(
        on_device, mesh=mesh, in_specs=in_specs, out_specs=out_specs, check_vma=False
    )
```

profile of v0, /device:TPU:1, one launch (start us, length us, event | category | flops | bytes accessed | tf_op | source)
XLA Modules:
  0.0 368.1 jit_solution(18234617934679933638)
XLA Ops:
  7.2 4.6 %copy.8 = bf16[8,4,256,256]{3,2,0,1:T(8,128)(2,1)} copy(bf16[8,4,256,256]{3,2,1,0:T(8,128)(2,1)} %param.8) | data formatting | bytes 8388608 | tf_op args[0]
  11.8 0.0 copy-start
  11.8 0.0 copy-start.2
  11.8 5.6 %all-to-all-start = ((bf16[8,4,256,256]{3,2,0,1:T(8,128)(2,1)}), bf16[8,4,256,256]{3,2,0,1:T(8,128)(2,1)}, u32[]{:S(2)}, u32[]{:S(2)}) async-start(bf16[8,4,256,256]{3,2,0,1:T(8,128)(2,1)} %copy.8), calls=%async_computation | async-start | bytes 8388608 | tf_op jit(solution)/shard_map/all_to_all | solution.py:58
  17.3 0.0 all-reduce.8.cloned.1.call-start
  18.0 0.0 copy-done
  18.0 0.7 multiply_reduce_fusion.2
  18.7 71.1 %psum.146 = f32[]{:T(128)} all-reduce(f32[]{:T(128)} %multiply_reduce_fusion.2), channel_id=1, replica_groups=mesh['groups'=2,'sector'=4,'op'=4] {'sector'}, use_global_device_ids=true, to_apply=%region_1.0 | all-reduce | flops 1 | bytes 8 | tf_op jit(solution)/shard_map/psum | solution.py:40
  90.6 0.1 divide_convert_fusion.2
  90.7 23.7 %collective-permute-start.1 = (bf16[1,256,256]{2,1,0:T(8,128)(2,1)S(1)}, bf16[1,256,256]{2,1,0:T(8,128)(2,1)S(1)}, u32[]{:S(2)}, u32[]{:S(2)}) collective-permute-start(bf16[1,256,256]{2,1,0:T(8,128)(2,1)S(1)} %divide_convert_fusion.2), channel_id=1, source_target_pairs={{0,4},{4,8},{8,12},{1,5},{5,9},{9,13},{2,6},{6,10},{10,14},{3,7},{... | collective-permute-start | bytes 393224 | tf_op jit(solution)/shard_map/ppermute | solution.py:12
  114.3 1.3 collective-permute-start
  115.6 0.0 copy-done.2
  115.7 0.1 reshape.128
  115.8 0.1 add.86
  115.9 0.1 fusion.86
  116.0 0.2 collective-permute-done.1
  116.3 4.0 %collective-permute-done = bf16[1,256,256]{2,1,0:T(8,128)(2,1)S(1)} collective-permute-done((bf16[1,256,256]{2,1,0:T(8,128)(2,1)S(1)}, bf16[1,256,256]{2,1,0:T(8,128)(2,1)S(1)}, u32[]{:S(2)}, u32[]{:S(2)}) %collective-permute-start) | collective-permute-done | bytes 131104 | tf_op jit(solution)/shard_map/ppermute | solution.py:15
  120.3 2.8 gather_fusion
  123.1 0.0 all-to-all-done
  123.1 0.0 copy-start.1
  123.1 7.9 %fusion.33 = f32[1,256,256]{2,1,0:T(8,128)} fusion(bf16[32,256,256]{2,1,0:T(8,128)(2,1)} %bitcast.131, bf16[32,256,256]{2,1,0:T(8,128)(2,1)} %bitcast.9, bf16[32,256,256]{2,1,0:T(8,128)(2,1)} %gather_fusion, pred[32]{0:T(512)(128)(4,1)S(1)} %compare_and_fusion), kind=kOutput, calls=%fused_computation.27 | convolution fusion | flops 2151677952 | bytes 12845088 | tf_op jit(solution)/shard_map/ktac,ktdc->tad/dot_general | solution.py:48
  131.1 0.0 all-reduce.8.cloned.1.call-update
  131.1 0.0 all-reduce.10.cloned.1.call-start
  131.1 33.4 %all-reduce.8.cloned.1.call-done = f32[1,256,256]{2,1,0:T(8,128)} async-done(((f32[1,256,256]{2,1,0:T(8,128)}), f32[1,256,256]{2,1,0:T(8,128)}) %all-reduce.8.cloned.1.call-update) | async-done | bytes 262160 | tf_op jit(solution)/shard_map/psum | solution.py:51
  164.6 0.0 copy-done.1
  164.6 1.7 fusion.63
  166.3 10.7 %all-reduce.3 = (f32[]{:T(128)}, f32[]{:T(128)}) all-reduce(f32[]{:T(128)} %get-tuple-element.23, f32[]{:T(128)} %get-tuple-element.22), channel_id=1, replica_groups=mesh['groups'=2,'sector'=4,'op'=4] {'sector'}, use_global_device_ids=true, to_apply=%region_4.6 | all-reduce | flops 2 | bytes 16 | tf_op jit(solution)/shard_map/psum | solution.py:40
  178.2 0.8 fusion.66
  179.0 7.2 %psum.150 = f32[]{:T(128)} all-reduce(f32[]{:T(128)} %get-tuple-element.40), channel_id=1, replica_groups=mesh['groups'=2,'sector'=4,'op'=4] {'sector'}, use_global_device_ids=true, to_apply=%region_8.10 | all-reduce | flops 1 | bytes 8 | tf_op jit(solution)/shard_map/psum | solution.py:40
  187.6 0.8 multiply_reduce_fusion.1
  188.4 8.7 %psum.151 = f32[]{:T(128)} all-reduce(f32[]{:T(128)} %multiply_reduce_fusion.1), channel_id=1, replica_groups=mesh['groups'=2,'sector'=4,'op'=4] {'sector'}, use_global_device_ids=true, to_apply=%region_10.12 | all-reduce | flops 1 | bytes 8 | tf_op jit(solution)/shard_map/psum | solution.py:40
  197.8 0.1 divide_convert_fusion.1
  197.9 1.9 collective-permute-start.3
  199.8 1.3 collective-permute-start.2
  201.1 0.7 collective-permute-done.3
  201.7 3.7 %collective-permute-done.2 = bf16[1,256,256]{2,1,0:T(8,128)(2,1)S(1)} collective-permute-done((bf16[1,256,256]{2,1,0:T(8,128)(2,1)S(1)}, bf16[1,256,256]{2,1,0:T(8,128)(2,1)S(1)}, u32[]{:S(2)}, u32[]{:S(2)}) %collective-permute-start.2) | collective-permute-done | bytes 131104 | tf_op jit(solution)/shard_map/ppermute | solution.py:15
  205.5 2.8 gather_fusion.1
  208.3 7.9 %fusion.38 = f32[1,256,256]{2,1,0:T(8,128)} fusion(bf16[32,256,256]{2,1,0:T(8,128)(2,1)} %bitcast.132, bf16[32,256,256]{2,1,0:T(8,128)(2,1)} %bitcast.9, bf16[32,256,256]{2,1,0:T(8,128)(2,1)} %gather_fusion.1, pred[32]{0:T(512)(128)(4,1)S(1)} %compare_and_fusion), kind=kOutput, calls=%fused_computation.28 | convolution fusion | flops 2151677952 | bytes 12845088 | tf_op jit(solution)/shard_map/ktac,ktdc->tad/dot_general | solution.py:48
  216.2 0.0 all-reduce.10.cloned.1.call-update
  216.2 0.0 all-reduce.12.cloned.1.call-start
  216.3 36.2 %all-reduce.10.cloned.1.call-done = f32[1,256,256]{2,1,0:T(8,128)} async-done(((f32[1,256,256]{2,1,0:T(8,128)}), f32[1,256,256]{2,1,0:T(8,128)}) %all-reduce.10.cloned.1.call-update) | async-done | bytes 262160 | tf_op jit(solution)/shard_map/psum | solution.py:51
  252.5 1.7 fusion.54
  254.2 10.7 %all-reduce.2 = (f32[]{:T(128)}, f32[]{:T(128)}) all-reduce(f32[]{:T(128)} %get-tuple-element.21, f32[]{:T(128)} %get-tuple-element.20), channel_id=1, replica_groups=mesh['groups'=2,'sector'=4,'op'=4] {'sector'}, use_global_device_ids=true, to_apply=%region_13.15 | all-reduce | flops 2 | bytes 16 | tf_op jit(solution)/shard_map/psum | solution.py:40
  266.2 0.8 fusion.68
  267.0 7.3 %all-reduce.1 = (f32[]{:T(128)}, f32[]{:T(128)}) all-reduce(f32[]{:T(128)} %get-tuple-element.19, f32[]{:T(128)} %get-tuple-element.18), channel_id=1, replica_groups=mesh['groups'=2,'sector'=4,'op'=4] {'sector'}, use_global_device_ids=true, to_apply=%region_19.21 | all-reduce | flops 2 | bytes 16 | tf_op jit(solution)/shard_map/psum | solution.py:40
  277.0 0.8 multiply_reduce_fusion
  277.8 8.7 %psum.157 = f32[]{:T(128)} all-reduce(f32[]{:T(128)} %multiply_reduce_fusion), channel_id=1, replica_groups=mesh['groups'=2,'sector'=4,'op'=4] {'sector'}, use_global_device_ids=true, to_apply=%region_21.23 | all-reduce | flops 1 | bytes 8 | tf_op jit(solution)/shard_map/psum | solution.py:40
  287.1 0.2 divide_convert_fusion
  287.3 1.9 collective-permute-start.5
  289.2 1.5 collective-permute-start.4
  290.7 0.5 collective-permute-done.5
  291.2 3.7 %collective-permute-done.4 = bf16[1,256,256]{2,1,0:T(8,128)(2,1)S(1)} collective-permute-done((bf16[1,256,256]{2,1,0:T(8,128)(2,1)S(1)}, bf16[1,256,256]{2,1,0:T(8,128)(2,1)S(1)}, u32[]{:S(2)}, u32[]{:S(2)}) %collective-permute-start.4) | collective-permute-done | bytes 131104 | tf_op jit(solution)/shard_map/ppermute | solution.py:15
  294.9 2.8 gather_fusion.2
  297.7 7.9 %fusion.43 = f32[1,256,256]{2,1,0:T(8,128)} fusion(bf16[32,256,256]{2,1,0:T(8,128)(2,1)} %bitcast.133, bf16[32,256,256]{2,1,0:T(8,128)(2,1)} %bitcast.9, bf16[32,256,256]{2,1,0:T(8,128)(2,1)} %gather_fusion.2, pred[32]{0:T(512)(128)(4,1)S(1)} %compare_and_fusion), kind=kOutput, calls=%fused_computation.29 | convolution fusion | flops 2151677952 | bytes 12845088 | tf_op jit(solution)/shard_map/ktac,ktdc->tad/dot_general | solution.py:48
  305.6 0.0 all-reduce.12.cloned.1.call-update
  305.6 36.3 %all-reduce.12.cloned.1.call-done = f32[1,256,256]{2,1,0:T(8,128)} async-done(((f32[1,256,256]{2,1,0:T(8,128)}), f32[1,256,256]{2,1,0:T(8,128)}) %all-reduce.12.cloned.1.call-update) | async-done | bytes 262160 | tf_op jit(solution)/shard_map/psum | solution.py:51
  341.9 2.6 fusion.49
  344.5 10.7 %all-reduce = (f32[1]{0:T(128)}, f32[1]{0:T(128)}, f32[1]{0:T(128)}, f32[1]{0:T(128)}, f32[1]{0:T(128)}, /*index=5*/f32[1]{0:T(128)}, f32[1]{0:T(128)}) all-reduce(f32[1]{0:T(128)} %bitcast.35, f32[1]{0:T(128)} %bitcast.36, f32[1]{0:T(128)} %bitcast.37, f32[1]{0:T(128)} %bitcast.39, ...), channel_id=1, replica_groups=mesh['groups'=2,'sector'=4,'op'=4] {'sector'}, use_global_device_ids=true, to_apply=%region_24.26 | all-reduce | flops 7 | bytes 56 | tf_op jit(solution)/shard_map/psum | solution.py:40
  355.2 5.7 %stack.87 = f32[9]{0:T(128)S(1)} concatenate(f32[1]{0:T(128)} %bitcast.34, f32[1]{0:T(128)} %get-tuple-element.24, f32[1]{0:T(128)} %get-tuple-element.25, f32[1]{0:T(128)} %get-tuple-element.26, f32[1]{0:T(128)} %bitcast.38, f32[1]{0:T(128)} %get-tuple-element.27, f32[1]{0:T(128)} %get-tuple-element.28, f32[1]{0:T(128)} %get-tuple-element.29, f32[1]{0:T(128)} %get-tuple-element.30), dimensions={0} | concatenate | bytes 72 | tf_op jit(solution)/shard_map/stack | solution.py:97
  360.9 0.7 div.70
  (9 shorter events, 0.2 us)
Async XLA Ops:
  11.8 6.2 %copy-start = (bf16[1,256,256]{2,1,0:T(8,128)(2,1)S(1)}, bf16[1,256,256]{2,1,0:T(8,128)(2,1)}, u32[]{:S(2)}) copy-start(bf16[1,256,256]{2,1,0:T(8,128)(2,1)} %param.12) | copy-start | bytes 393220
  11.8 103.9 %copy-start.2 = (s32[128]{0:T(128)S(1)}, s32[128]{0:T(128)}, u32[]{:S(2)}) copy-start(s32[128]{0:T(128)} %param.10) | copy-start | bytes 1540
  11.8 111.4 %all-to-all-start = ((bf16[8,4,256,256]{3,2,0,1:T(8,128)(2,1)}), bf16[8,4,256,256]{3,2,0,1:T(8,128)(2,1)}, u32[]{:S(2)}, u32[]{:S(2)}) async-start(bf16[8,4,256,256]{3,2,0,1:T(8,128)(2,1)} %copy.8), calls=%async_computation | async-start | bytes 8388608 | tf_op jit(solution)/shard_map/all_to_all | solution.py:58
  17.3 147.3 %all-reduce.8.cloned.1.call-start = ((), (), s32[]{:S(2)}) async-start(), calls=%async_computation.1 | async-start | bytes 524288 | tf_op jit(solution)/shard_map/psum | solution.py:51
  90.7 25.6 %collective-permute-start.1 = (bf16[1,256,256]{2,1,0:T(8,128)(2,1)S(1)}, bf16[1,256,256]{2,1,0:T(8,128)(2,1)S(1)}, u32[]{:S(2)}, u32[]{:S(2)}) collective-permute-start(bf16[1,256,256]{2,1,0:T(8,128)(2,1)S(1)} %divide_convert_fusion.2), channel_id=1, source_target_pairs={{0,4},{4,8},{8,12},{1,5},{5,9},{9,13},{2,6},{6,10},{10,14},{3,7},{... | collective-permute-start | bytes 393224 | tf_op jit(solution)/shard_map/ppermute | solution.py:12
  114.3 6.0 %collective-permute-start = (bf16[1,256,256]{2,1,0:T(8,128)(2,1)S(1)}, bf16[1,256,256]{2,1,0:T(8,128)(2,1)S(1)}, u32[]{:S(2)}, u32[]{:S(2)}) collective-permute-start(bf16[1,256,256]{2,1,0:T(8,128)(2,1)S(1)} %divide_convert_fusion.2), channel_id=1, source_target_pairs={{4,0},{8,4},{12,8},{5,1},{9,5},{13,9},{6,2},{10,6},{14,10},{7,3},{... | collective-permute-start | bytes 393224 | tf_op jit(solution)/shard_map/ppermute | solution.py:15
  123.1 41.4 %copy-start.1 = (f32[1,256,256]{2,1,0:T(8,128)S(1)}, f32[1,256,256]{2,1,0:T(8,128)}, u32[]{:S(2)}) copy-start(f32[1,256,256]{2,1,0:T(8,128)} %param.13) | copy-start | bytes 786436
  131.1 121.4 %all-reduce.10.cloned.1.call-start = ((), (), s32[]{:S(2)}) async-start(), calls=%async_computation.2 | async-start | bytes 524288 | tf_op jit(solution)/shard_map/psum | solution.py:51
  197.9 3.8 %collective-permute-start.3 = (bf16[1,256,256]{2,1,0:T(8,128)(2,1)S(1)}, bf16[1,256,256]{2,1,0:T(8,128)(2,1)S(1)}, u32[]{:S(2)}, u32[]{:S(2)}) collective-permute-start(bf16[1,256,256]{2,1,0:T(8,128)(2,1)S(1)} %divide_convert_fusion.1), channel_id=1, source_target_pairs={{0,4},{4,8},{8,12},{1,5},{5,9},{9,13},{2,6},{6,10},{10,14},{3,7},{... | collective-permute-start | bytes 393224 | tf_op jit(solution)/shard_map/ppermute | solution.py:12
  199.8 5.7 %collective-permute-start.2 = (bf16[1,256,256]{2,1,0:T(8,128)(2,1)S(1)}, bf16[1,256,256]{2,1,0:T(8,128)(2,1)S(1)}, u32[]{:S(2)}, u32[]{:S(2)}) collective-permute-start(bf16[1,256,256]{2,1,0:T(8,128)(2,1)S(1)} %divide_convert_fusion.1), channel_id=1, source_target_pairs={{4,0},{8,4},{12,8},{5,1},{9,5},{13,9},{6,2},{10,6},{14,10},{7,3},{... | collective-permute-start | bytes 393224 | tf_op jit(solution)/shard_map/ppermute | solution.py:15
  216.2 125.7 %all-reduce.12.cloned.1.call-start = ((), (), s32[]{:S(2)}) async-start(), calls=%async_computation.3 | async-start | bytes 524288 | tf_op jit(solution)/shard_map/psum | solution.py:51
  287.3 3.8 %collective-permute-start.5 = (bf16[1,256,256]{2,1,0:T(8,128)(2,1)S(1)}, bf16[1,256,256]{2,1,0:T(8,128)(2,1)S(1)}, u32[]{:S(2)}, u32[]{:S(2)}) collective-permute-start(bf16[1,256,256]{2,1,0:T(8,128)(2,1)S(1)} %divide_convert_fusion), channel_id=1, source_target_pairs={{0,4},{4,8},{8,12},{1,5},{5,9},{9,13},{2,6},{6,10},{10,14},{3,7},{... | collective-permute-start | bytes 393224 | tf_op jit(solution)/shard_map/ppermute | solution.py:12
  289.2 5.7 %collective-permute-start.4 = (bf16[1,256,256]{2,1,0:T(8,128)(2,1)S(1)}, bf16[1,256,256]{2,1,0:T(8,128)(2,1)S(1)}, u32[]{:S(2)}, u32[]{:S(2)}) collective-permute-start(bf16[1,256,256]{2,1,0:T(8,128)(2,1)S(1)} %divide_convert_fusion), channel_id=1, source_target_pairs={{4,0},{8,4},{12,8},{5,1},{9,5},{13,9},{6,2},{10,6},{14,10},{7,3},{... | collective-permute-start | bytes 393224 | tf_op jit(solution)/shard_map/ppermute | solution.py:15
Sparse Core Ops, SparseCore 0:
  131.2 33.3 all-reduce.7
  216.4 36.1 all-reduce.9
  305.8 36.1 all-reduce.11
where the time goes:
time: 373 us; the launch traced here: 368 us
  blocking collectives  135 us (36%)
  waiting for transfers between devices  119 us (32%)
  starting transfers between devices  37.1 us (10%)
  matrix products  23.7 us (6%)
  between operations  23.2 us (6%)
  local copies, waits for them, and re-layouts  19.5 us (5%)
  other arithmetic  10.6 us (3%)
    psum x8, blocking collectives, total_sums(): return lax.psum(values, 'sector')  135 us
    psum x3, waiting for transfers between devices, finish(): summed = lax.psum(partial_image, 'op')  106 us
    ppermute x3, starting transfers between devices, with_halo(): lax.ppermute(lax.slice_in_dim(block, block.shape[dim] - width, None, axis...  27.4 us
    dot_general x3, matrix products, finish(): jnp.einsum('ktac,ktdc->tad', middle_portion, right_local, preferred_eleme...  23.7 us
    ppermute x3, waiting for transfers between devices, with_halo(): lax.ppermute(lax.slice_in_dim(block, 0, width, axis=dim), axis, backward)  11.5 us
    gather x3, local copies, waits for them, and re-layouts, sources(): return jnp.take(shifted, charges + 1, axis=0)  8.36 us
  transfers between devices with their start and end apart: 10, of which 9 were waited for; matrix products, arithmetic and copies ran while one was open for 1% of the time, Pallas kernels for 0%

commit v1 on v0

v1 whole, which is shorter than its diff:
```python
import functools

import jax
import jax.numpy as jnp
from jax import lax
from jax.experimental import pallas as pl
from jax.experimental.pallas import tpu as pltpu
from jax.sharding import PartitionSpec as P

F32 = jnp.float32
BF16 = jnp.bfloat16
LANES = 128
MESH = pl.DeviceIdType.MESH


def fold(values):
    row = jnp.sum(values, axis=0, keepdims=True)
    total = row[:, :LANES]
    for start in range(LANES, row.shape[1], LANES):
        total = total + row[:, start : start + LANES]
    return total


def davidson_kernel(
    sectors, ops,
    left_ref, right_ref, charge_ref, dims_ref, wave_ref, onsite_ref,
    image_ref, corr_ref,
    lbuf, rbuf, pbuf, acc, v0, v1, v2, part_send, part_recv, full, tiles,
    left_local, right_local, left_send, left_recv, v_send, v_recv,
    part_send_sem, part_recv_sem, tile_send, tile_recv, full_send, full_recv,
):
    held = (v0, v1, v2)
    t = lax.axis_index("sector")
    q = lax.axis_index("op")
    me = t * ops + q
    peers = sectors * ops
    per = left_ref.shape[0]
    states = wave_ref.shape[1]
    quarter = states // ops
    blocks = sectors * per
    entries = sectors * states * states

    def rows_of(index):
        return pl.ds(pl.multiple_of(index * quarter, quarter), quarter)

    mine = rows_of(q)

    def device(s, o):
        return {"sector": s, "op": o}

    barrier = pltpu.get_barrier_semaphore()

    def greet(p, carry):
        other = lax.rem(me + p, peers)
        pl.semaphore_signal(
            barrier, inc=1, device_id=device(other // ops, lax.rem(other, ops)),
            device_id_type=MESH,
        )
        return carry

    lax.fori_loop(1, peers, greet, 0)

    right_copy = pltpu.make_async_copy(right_ref, rbuf, right_local)
    right_copy.start()
    own_copy = pltpu.make_async_copy(
        left_ref.at[:, t], lbuf.at[pl.ds(t * per, per)], left_local
    )
    own_copy.start()
    pl.semaphore_wait(barrier, peers - 1)

    def left_copy(k, p):
        target = lax.rem(t + p, sectors)
        return pltpu.make_async_remote_copy(
            src_ref=left_ref.at[k, target],
            dst_ref=lbuf.at[t * per + k],
            send_sem=left_send.at[p, k],
            recv_sem=left_recv.at[t, k],
            device_id=device(target, q),
            device_id_type=MESH,
        )

    def left_arrives(k, p):
        source = lax.rem(t + p, sectors)
        return source * per + k, pltpu.make_async_remote_copy(
            src_ref=left_ref.at[k, source],
            dst_ref=lbuf.at[source * per + k],
            send_sem=left_send.at[p, k],
            recv_sem=left_recv.at[source, k],
            device_id=device(source, q),
            device_id_type=MESH,
        )

    remote_blocks = per * (sectors - 1)

    def send_left(i, carry):
        left_copy(i // (sectors - 1), lax.rem(i, sectors - 1) + 1).start()
        return carry

    lax.fori_loop(0, remote_blocks, send_left, 0)

    def tile_copy(turn, p):
        other = lax.rem(me + p, peers)
        return other, pltpu.make_async_remote_copy(
            src_ref=tiles.at[turn, me],
            dst_ref=tiles.at[turn, me],
            send_sem=tile_send.at[turn, p],
            recv_sem=tile_recv.at[turn, me],
            device_id=device(other // ops, lax.rem(other, ops)),
            device_id_type=MESH,
        )

    def send_sums(turn, rows):
        rows = list(rows) + [jnp.zeros((8 - len(rows), LANES), F32)]
        tiles[turn, me] = jnp.concatenate(rows, axis=0)

        def step(p, carry):
            tile_copy(turn, p)[1].start()
            return carry

        lax.fori_loop(1, peers, step, 0)

    def take_sums(turn):
        def step(p, carry):
            other, copy = tile_copy(turn, p)
            pltpu.make_async_remote_copy(
                src_ref=tiles.at[turn, other],
                dst_ref=tiles.at[turn, other],
                send_sem=tile_send.at[turn, p],
                recv_sem=tile_recv.at[turn, other],
                device_id=device(other // ops, lax.rem(other, ops)),
                device_id_type=MESH,
            ).wait_recv()
            copy.wait_send()
            return carry

        lax.fori_loop(1, peers, step, 0)
        total = jnp.sum(jnp.sum(tiles[turn], axis=0), axis=1, keepdims=True)
        return [total[i : i + 1, :] for i in range(8)]

    def vector_copy(j, d, o, source):
        return pltpu.make_async_remote_copy(
            src_ref=held[j].at[1, mine],
            dst_ref=held[j].at[d + 1, rows_of(source)],
            send_sem=v_send.at[j, d + 1, o],
            recv_sem=v_recv.at[j, d + 1, source],
            device_id=device(t + d, o),
            device_id_type=MESH,
        )

    def each_reader(action):
        for d in (1, -1, 0):
            def run(d=d):
                def step(p, carry):
                    action(d, lax.rem(q + p, ops))
                    return carry

                lax.fori_loop(1 if d == 0 else 0, ops, step, 0)

            if d == 0:
                run()
            else:
                pl.when((t + d >= 0) & (t + d < sectors))(run)

    def send_vector(j, values):
        held[j][1, mine] = values
        each_reader(lambda d, o: vector_copy(j, d, o, q).start())

    def take_vector(j):
        each_reader(lambda d, o: vector_copy(j, -d, o, o).wait_recv())
        each_reader(lambda d, o: vector_copy(j, d, o, q).wait_send())

    for j in range(3):
        @pl.when(t == 0)
        def _(j=j):
            held[j][2] = jnp.zeros((states, states), BF16)

        @pl.when(t == sectors - 1)
        def _(j=j):
            held[j][0] = jnp.zeros((states, states), BF16)

    dims = dims_ref[0]
    row_at = lax.broadcasted_iota(jnp.int32, (quarter, states), 0) + q * quarter
    column_at = lax.broadcasted_iota(jnp.int32, (quarter, states), 1)
    mask = ((row_at < dims) & (column_at < dims)).astype(F32)
    onsite = onsite_ref[0, mine]

    masked = mask * wave_ref[0, mine].astype(F32)
    send_sums(0, [fold(masked * masked)])
    start_norm = take_sums(0)[0]
    vector = (masked / jnp.sqrt(start_norm / entries + 1e-06)).astype(BF16)
    send_vector(0, vector)
    right_copy.wait()
    own_copy.wait()

    def right_products(j):
        def step(i, carry):
            charge = charge_ref[(i // per * ops + q) * per + lax.rem(i, per)]
            pbuf[i] = lax.dot_general(
                held[j][charge + 1], rbuf[i], (((1,), (1,)), ((), ())),
                preferred_element_type=F32,
            ).astype(BF16)
            return carry

        lax.fori_loop(0, blocks, step, 0, unroll=4)

    def product(i):
        return jnp.dot(lbuf[i], pbuf[i], preferred_element_type=F32)

    group = 4 if blocks % 4 == 0 else 1

    def left_products(arriving):
        acc[...] = jnp.zeros_like(acc)
        if arriving:
            def own(k, carry):
                acc[...] += product(t * per + k)
                return carry

            lax.fori_loop(0, per, own, 0)

            def step(i, carry):
                at, copy = left_arrives(i // (sectors - 1), lax.rem(i, sectors - 1) + 1)
                copy.wait_recv()
                acc[...] += product(at)
                return carry

            lax.fori_loop(0, remote_blocks, step, 0)
        else:
            def step(i, carry):
                total = product(i * group)
                for n in range(1, group):
                    total = total + product(i * group + n)
                acc[...] += total
                return carry

            lax.fori_loop(0, blocks // group, step, 0)

    def part_copy(j, o, source):
        return pltpu.make_async_remote_copy(
            src_ref=part_send.at[j, rows_of(o)],
            dst_ref=part_recv.at[j, source],
            send_sem=part_send_sem.at[j, o],
            recv_sem=part_recv_sem.at[j, source],
            device_id=device(t, o),
            device_id_type=MESH,
        )

    def each_op(action):
        def step(p, carry):
            action(lax.rem(q + p, ops))
            return carry

        lax.fori_loop(1, ops, step, 0)

    def send_partial(j):
        part_send[j] = acc[...].astype(BF16)
        each_op(lambda o: part_copy(j, o, q).start())

    def take_partial(j, vector):
        part_recv[j, q] = part_send[j, mine]
        each_op(lambda o: part_copy(j, o, o).wait_recv())
        each_op(lambda o: part_copy(j, o, q).wait_send())
        total = acc[mine]
        own = part_recv[j, q].astype(F32)
        total = total + (jnp.sum(part_recv[j].astype(F32), axis=0) - own)
        return mask * (onsite * vector.astype(F32) + total)

    vectors = [vector]
    images = []
    norms = []
    ritz = []
    cross = []
    for j in range(3):
        current = vectors[j].astype(F32)
        take_vector(j)
        right_products(j)
        left_products(j == 0)
        send_partial(j)
        diagonal = onsite * current

        def overlap(i):
            whole = fold(held[i][1].astype(F32) * acc[...])
            return whole + fold(vectors[i].astype(F32) * diagonal)

        if j == 0:
            rows = [overlap(0), fold(current * current)]
        elif j == 1:
            first = vectors[0].astype(F32)
            rows = [
                overlap(1), fold(current * current), overlap(0),
                fold(current * images[0]), fold(first * current),
            ]
        else:
            rows = [
                overlap(2), overlap(0), overlap(1),
                fold(current * images[0]), fold(current * images[1]),
            ]
        send_sums(1 + 2 * j, rows)
        image = take_partial(j, vectors[j])
        images.append(image)
        if j == 2:
            break
        sums = take_sums(1 + 2 * j)
        ritz.append(sums)
        norms.append(sums[1])
        rayleigh = sums[0] / sums[1]
        correction = (image - rayleigh * current) / (1.0 + jnp.abs(onsite - rayleigh))
        send_sums(
            2 + 2 * j,
            [fold(correction * correction)]
            + [fold(older.astype(F32) * correction) for older in vectors],
        )
        seconds = take_sums(2 + 2 * j)
        length = seconds[0]
        update = correction
        factors = []
        for i in range(j + 1):
            factor = seconds[1 + i] / norms[i]
            factors.append(factor)
            update = update - factor * vectors[i].astype(F32)
            length = length - factor * seconds[1 + i]
        if j == 1:
            length = length + 2.0 * factors[0] * factors[1] * sums[4]
        length = jnp.maximum(length, 0.0)
        following = (update / jnp.sqrt(length / entries + 1e-06)).astype(BF16)
        vectors.append(following)
        send_vector(j + 1, following)

    full[mine] = images[2]

    def full_copy(o, source):
        return pltpu.make_async_remote_copy(
            src_ref=full.at[mine],
            dst_ref=full.at[rows_of(source)],
            send_sem=full_send.at[o],
            recv_sem=full_recv.at[source],
            device_id=device(t, o),
            device_id_type=MESH,
        )

    each_op(lambda o: full_copy(o, q).start())
    last = take_sums(5)
    values = [
        [ritz[0][0], ritz[1][2], last[1]],
        [ritz[1][3], ritz[1][0], last[2]],
        [last[3], last[4], last[0]],
    ]
    at_row = lax.broadcasted_iota(jnp.int32, (8, LANES), 0)
    at_column = lax.broadcasted_iota(jnp.int32, (8, LANES), 1)
    table = jnp.zeros((8, LANES), F32)
    for i in range(3):
        for n in range(3):
            table = jnp.where((at_row == i) & (at_column == n), values[i][n] / entries, table)
    corr_ref[...] = table[:3, :3]

    def sent_left(i, carry):
        left_copy(i // (sectors - 1), lax.rem(i, sectors - 1) + 1).wait_send()
        return carry

    lax.fori_loop(0, remote_blocks, sent_left, 0)
    each_op(lambda o: full_copy(o, o).wait_recv())
    each_op(lambda o: full_copy(o, q).wait_send())
    image_ref[0] = full[...]


def on_device(left_arrival, right_env, op_charge, sector_dims, wavefunction, onsite):
    sectors = lax.axis_size("sector")
    ops = lax.axis_size("op")
    per = left_arrival.shape[0]
    states = wavefunction.shape[1]
    blocks = sectors * per
    quarter = states // ops
    right = right_env.reshape(blocks, states, states)
    vmem = pl.BlockSpec(memory_space=pltpu.VMEM)
    smem = pl.BlockSpec(memory_space=pltpu.SMEM)
    anywhere = pl.BlockSpec(memory_space=pl.ANY)
    dma = pltpu.SemaphoreType.DMA
    return pl.pallas_call(
        functools.partial(davidson_kernel, sectors, ops),
        out_shape=(
            jax.ShapeDtypeStruct(wavefunction.shape, F32),
            jax.ShapeDtypeStruct((3, 3), F32),
        ),
        in_specs=[anywhere, anywhere, smem, smem, vmem, vmem],
        out_specs=(vmem, vmem),
        scratch_shapes=[
            pltpu.VMEM((blocks, states, states), BF16),
            pltpu.VMEM((blocks, states, states), BF16),
            pltpu.VMEM((blocks, states, states), BF16),
            pltpu.VMEM((states, states), F32),
            pltpu.VMEM((3, states, states), BF16),
            pltpu.VMEM((3, states, states), BF16),
            pltpu.VMEM((3, states, states), BF16),
            pltpu.VMEM((3, states, states), BF16),
            pltpu.VMEM((3, ops, quarter, states), BF16),
            pltpu.VMEM((states, states), F32),
            pltpu.VMEM((6, sectors * ops, 8, LANES), F32),
            dma,
            dma,
            dma((sectors, per)),
            dma((sectors, per)),
            dma((3, 3, ops)),
            dma((3, 3, ops)),
            dma((3, ops)),
            dma((3, ops)),
            dma((6, sectors * ops)),
            dma((6, sectors * ops)),
            dma((ops,)),
            dma((ops,)),
        ],
        compiler_params=pltpu.CompilerParams(
            collective_id=0, has_side_effects=True, vmem_limit_bytes=48 * 1024 * 1024
        ),
    )(left_arrival, right, op_charge, sector_dims, wavefunction, onsite)


def solution(mesh):
    in_specs = (
        P(("groups", "sector", "op"), None, None, None),
        P("groups", "op", None, "sector", None, None),
        P("groups"),
        P(("groups", "sector")),
        P(("groups", "sector"), None, None),
        P(("groups", "sector"), None, None),
    )
    out_specs = (P(("groups", "sector"), None, None), P("groups", None))
    return jax.shard_map(
        on_device, mesh=mesh, in_specs=in_specs, out_specs=out_specs, check_vma=False
    )
```

time: 373 us -> 171 us (0.46); the launches traced: 368 us -> 171 us
  Pallas kernels: 0 us -> 164 us
  blocking collectives: 135 us -> 0 us
  waiting for transfers between devices: 119 us -> 0 us
  starting transfers between devices: 37.1 us -> 0 us
  matrix products: 23.7 us -> 0 us
  between operations: 23.2 us -> 1.3 us
  local copies, waits for them, and re-layouts: 19.5 us -> 5.97 us
  other arithmetic: 10.6 us -> 0 us
    pallas_call x0 -> x1, Pallas kernels: none -> 164 us  [on_device(): pl.pallas_call(functools.partial(davidson_kernel, sectors, ops), out_shap...]
    psum x8 -> x0, blocking collectives: 135 us -> none  [total_sums(): return lax.psum(values, 'sector')]
    psum x3 -> x0, waiting for transfers between devices: 106 us -> none  [finish(): summed = lax.psum(partial_image, 'op')]
    ppermute x6 -> x0, starting transfers between devices: 31.4 us -> none  [the longest x3 27.4 us: with_halo(): lax.ppermute(lax.slice_in_dim(block, block.shape[dim] - width, None, axis...]
    dot_general x3 -> x0, matrix products: 23.7 us -> none  [finish(): jnp.einsum('ktac,ktdc->tad', middle_portion, right_local, preferred_eleme...]
    ppermute x6 -> x0, waiting for transfers between devices: 12.9 us -> none  [the longest x3 11.5 us: with_halo(): lax.ppermute(lax.slice_in_dim(block, 0, width, axis=dim), axis, backward)]
    reduce_sum x8 -> x0, other arithmetic: 9.91 us -> none  [the longest x2 3.45 us: on_device(): ritz = total_sums((jnp.sum(current * image), jnp.sum(current * current)))]
    gather x3 -> x0, local copies, waits for them, and re-layouts: 8.36 us -> none  [sources(): return jnp.take(shifted, charges + 1, axis=0)]
  transfers between devices with their start and end apart: 10 -> 0, of which waited for: 9 -> 0; matrix products, arithmetic and copies ran while one was open for 1% -> 0% of each run, Pallas kernels for 0% -> 0%
where the time goes in v1:
time: 171 us
  Pallas kernels  164 us (96%)
  local copies, waits for them, and re-layouts  5.97 us (3%)
    pallas_call x1, Pallas kernels, on_device(): pl.pallas_call(functools.partial(davidson_kernel, sectors, ops), out_shap...  164 us
    unnamed x10, local copies, waits for them, and re-layouts  5.97 us

profile of v1, /device:TPU:1, one launch (start us, length us, event | category | flops | bytes accessed | tf_op | source)
XLA Modules:
  0.0 171.2 jit_solution(11009074258750264619)
XLA Ops:
  1.3 0.0 copy-start
  1.3 2.2 %copy-done = bf16[8,4,256,256]{3,2,1,0:T(8,128)(2,1)S(1)} copy-done((bf16[8,4,256,256]{3,2,1,0:T(8,128)(2,1)S(1)}, bf16[8,4,256,256]{3,2,1,0:T(8,128)(2,1)}, u32[]{:S(2)}) %copy-start) | copy-done | bytes 4194328
  3.5 0.0 copy-start.1
  3.5 0.9 copy-done.1
  4.4 0.0 copy-start.2
  4.4 0.9 copy-done.2
  5.3 0.0 copy-start.3
  5.3 0.7 copy-done.3
  6.0 163.9 %shard_map.77 = (f32[1,256,256]{2,1,0:T(8,128)S(1)}, f32[3,3]{1,0:T(4,128)S(1)}) custom-call(bf16[8,4,256,256]{3,2,1,0:T(8,128)(2,1)S(1)} %copy-done, bf16[32,256,256]{2,1,0:T(8,128)(2,1)} %bitcast.1, s32[128]{0:T(128)S(1)} %copy-done.3, s32[1]{0:T(128)S(6)} %copy.10.dims_ref, bf16[1,256,256]{2,1,0:T(8,128)(2,1)S(1)} %copy-done.2, f32[1,256,256]{2,1,0:T(8,128)S(1)} %copy-done.1), custom_call_target="tpu_custom_call" | custom-call | tf_op jit(solution)/shard_map/pallas_call | solution.py:377
  169.9 0.7 copy.11
  170.6 0.6 copy.12
Async XLA Ops:
  1.3 2.2 %copy-start = (bf16[8,4,256,256]{3,2,1,0:T(8,128)(2,1)S(1)}, bf16[8,4,256,256]{3,2,1,0:T(8,128)(2,1)}, u32[]{:S(2)}) copy-start(bf16[8,4,256,256]{3,2,1,0:T(8,128)(2,1)} %left_ref.1) | copy-start | bytes 12582916
  3.5 0.9 copy-start.1
  4.4 0.9 copy-start.2
  5.3 0.7 copy-start.3

commit v2 on v1

--- a/solution.py
+++ b/solution.py
@@ -23,9 +23,9 @@
 
 def davidson_kernel(
     sectors, ops,
-    left_ref, right_ref, charge_ref, dims_ref, wave_ref, onsite_ref,
+    left_ref, right_ref, charge_hbm, dims_hbm, wave_hbm, onsite_hbm,
     image_ref, corr_ref,
-    lbuf, rbuf, pbuf, acc, v0, v1, v2, part_send, part_recv, full, tiles,
+    charge_ref, dims_ref, wave_ref, onsite_ref, small_local, lbuf, rbuf, pbuf, acc, v0, v1, v2, part_send, part_recv, full, tiles,
     left_local, right_local, left_send, left_recv, v_send, v_recv,
     part_send_sem, part_recv_sem, tile_send, tile_recv, full_send, full_recv,
 ):
@@ -35,7 +35,7 @@
     me = t * ops + q
     peers = sectors * ops
     per = left_ref.shape[0]
-    states = wave_ref.shape[1]
+    states = wave_hbm.shape[1]
     quarter = states // ops
     blocks = sectors * per
     entries = sectors * states * states
@@ -47,6 +47,16 @@
 
     def device(s, o):
         return {"sector": s, "op": o}
+
+    small_copies = [
+        pltpu.make_async_copy(source, target, small_local.at[i])
+        for i, (source, target) in enumerate((
+            (dims_hbm, dims_ref), (wave_hbm, wave_ref), (onsite_hbm, onsite_ref),
+            (charge_hbm, charge_ref),
+        ))
+    ]
+    for copy in small_copies:
+        copy.start()
 
     barrier = pltpu.get_barrier_semaphore()
 
@@ -58,7 +68,7 @@
         )
         return carry
 
-    lax.fori_loop(1, peers, greet, 0)
+    lax.fori_loop(1, peers, greet, 0, unroll=peers <= 16)
 
     right_copy = pltpu.make_async_copy(right_ref, rbuf, right_local)
     right_copy.start()
@@ -66,7 +76,6 @@
         left_ref.at[:, t], lbuf.at[pl.ds(t * per, per)], left_local
     )
     own_copy.start()
-    pl.semaphore_wait(barrier, peers - 1)
 
     def left_copy(k, p):
         target = lax.rem(t + p, sectors)
@@ -96,8 +105,6 @@
         left_copy(i // (sectors - 1), lax.rem(i, sectors - 1) + 1).start()
         return carry
 
-    lax.fori_loop(0, remote_blocks, send_left, 0)
-
     def tile_copy(turn, p):
         other = lax.rem(me + p, peers)
         return other, pltpu.make_async_remote_copy(
@@ -117,7 +124,7 @@
             tile_copy(turn, p)[1].start()
             return carry
 
-        lax.fori_loop(1, peers, step, 0)
+        lax.fori_loop(1, peers, step, 0, unroll=peers <= 16)
 
     def take_sums(turn):
         def step(p, carry):
@@ -133,7 +140,7 @@
             copy.wait_send()
             return carry
 
-        lax.fori_loop(1, peers, step, 0)
+        lax.fori_loop(1, peers, step, 0, unroll=peers <= 16)
         total = jnp.sum(jnp.sum(tiles[turn], axis=0), axis=1, keepdims=True)
         return [total[i : i + 1, :] for i in range(8)]
 
@@ -154,7 +161,7 @@
                     action(d, lax.rem(q + p, ops))
                     return carry
 
-                lax.fori_loop(1 if d == 0 else 0, ops, step, 0)
+                lax.fori_loop(1 if d == 0 else 0, ops, step, 0, unroll=True)
 
             if d == 0:
                 run()
@@ -178,6 +185,8 @@
         def _(j=j):
             held[j][0] = jnp.zeros((states, states), BF16)
 
+    for copy in small_copies:
+        copy.wait()
     dims = dims_ref[0]
     row_at = lax.broadcasted_iota(jnp.int32, (quarter, states), 0) + q * quarter
     column_at = lax.broadcasted_iota(jnp.int32, (quarter, states), 1)
@@ -185,10 +194,15 @@
     onsite = onsite_ref[0, mine]
 
     masked = mask * wave_ref[0, mine].astype(F32)
-    send_sums(0, [fold(masked * masked)])
+    first_sums = [fold(masked * masked)]
+    pl.semaphore_wait(barrier, peers - 1)
+    send_sums(0, first_sums)
+    early = min(2 * (sectors - 1), remote_blocks)
+    lax.fori_loop(0, early, send_left, 0)
     start_norm = take_sums(0)[0]
     vector = (masked / jnp.sqrt(start_norm / entries + 1e-06)).astype(BF16)
     send_vector(0, vector)
+    lax.fori_loop(early, remote_blocks, send_left, 0)
     right_copy.wait()
     own_copy.wait()
 
@@ -249,7 +263,7 @@
             action(lax.rem(q + p, ops))
             return carry
 
-        lax.fori_loop(1, ops, step, 0)
+        lax.fori_loop(1, ops, step, 0, unroll=True)
 
     def send_partial(j):
         part_send[j] = acc[...].astype(BF16)
@@ -371,7 +385,6 @@
     quarter = states // ops
     right = right_env.reshape(blocks, states, states)
     vmem = pl.BlockSpec(memory_space=pltpu.VMEM)
-    smem = pl.BlockSpec(memory_space=pltpu.SMEM)
     anywhere = pl.BlockSpec(memory_space=pl.ANY)
     dma = pltpu.SemaphoreType.DMA
     return pl.pallas_call(
@@ -380,9 +393,14 @@
             jax.ShapeDtypeStruct(wavefunction.shape, F32),
             jax.ShapeDtypeStruct((3, 3), F32),
         ),
-        in_specs=[anywhere, anywhere, smem, smem, vmem, vmem],
+        in_specs=[anywhere] * 6,
         out_specs=(vmem, vmem),
         scratch_shapes=[
+            pltpu.SMEM(op_charge.shape, jnp.int32),
+            pltpu.SMEM(sector_dims.shape, jnp.int32),
+            pltpu.VMEM(wavefunction.shape, BF16),
+            pltpu.VMEM(onsite.shape, F32),
+            dma((4,)),
             pltpu.VMEM((blocks, states, states), BF16),
             pltpu.VMEM((blocks, states, states), BF16),
             pltpu.VMEM((blocks, states, states), BF16),

time: 171 us -> 159 us (0.930)
  Pallas kernels: 164 us -> 151 us
    pallas_call x1, Pallas kernels: 164 us -> 151 us  [on_device(): pl.pallas_call(functools.partial(davidson_kernel, sectors, ops), out_shap...]
where the time goes in v2:
time: 159 us
  Pallas kernels  151 us (95%)
  local copies, waits for them, and re-layouts  5.97 us (4%)
    pallas_call x1, Pallas kernels, on_device(): pl.pallas_call(functools.partial(davidson_kernel, sectors, ops), out_shap...  151 us
    unnamed x10, local copies, waits for them, and re-layouts  5.97 us

profile of v2, /device:TPU:1, one launch (start us, length us, event | category | flops | bytes accessed | tf_op | source)
XLA Modules:
  0.0 158.7 jit_solution(1504206791414237479)
XLA Ops:
  1.3 0.0 copy-start
  1.3 2.2 %copy-done = bf16[8,4,256,256]{3,2,1,0:T(8,128)(2,1)S(1)} copy-done((bf16[8,4,256,256]{3,2,1,0:T(8,128)(2,1)S(1)}, bf16[8,4,256,256]{3,2,1,0:T(8,128)(2,1)}, u32[]{:S(2)}) %copy-start) | copy-done | bytes 4194328
  3.5 0.0 copy-start.1
  3.5 0.9 copy-done.1
  4.4 0.0 copy-start.2
  4.4 0.9 copy-done.2
  5.3 0.0 copy-start.3
  5.3 0.7 copy-done.3
  6.0 151.5 %shard_map.77 = (f32[1,256,256]{2,1,0:T(8,128)S(1)}, f32[3,3]{1,0:T(4,128)S(1)}) custom-call(bf16[8,4,256,256]{3,2,1,0:T(8,128)(2,1)S(1)} %copy-done, bf16[32,256,256]{2,1,0:T(8,128)(2,1)} %bitcast.1, s32[128]{0:T(128)S(1)} %copy-done.3, s32[1]{0:T(128)S(6)} %copy.10.dims_hbm, bf16[1,256,256]{2,1,0:T(8,128)(2,1)S(1)} %copy-done.2, f32[1,256,256]{2,1,0:T(8,128)S(1)} %copy-done.1), custom_call_target="tpu_custom_call" | custom-call | tf_op jit(solution)/shard_map/pallas_call | solution.py:390
  157.4 0.7 copy.11
  158.2 0.6 copy.12
Async XLA Ops:
  1.3 2.2 %copy-start = (bf16[8,4,256,256]{3,2,1,0:T(8,128)(2,1)S(1)}, bf16[8,4,256,256]{3,2,1,0:T(8,128)(2,1)}, u32[]{:S(2)}) copy-start(bf16[8,4,256,256]{3,2,1,0:T(8,128)(2,1)} %left_ref.1) | copy-start | bytes 12582916
  3.5 0.9 copy-start.1
  4.4 0.9 copy-start.2
  5.3 0.7 copy-start.3

commit v3 on v2

--- a/solution.py
+++ b/solution.py
@@ -215,12 +215,12 @@
             ).astype(BF16)
             return carry
 
-        lax.fori_loop(0, blocks, step, 0, unroll=4)
+        lax.fori_loop(0, blocks, step, 0, unroll=8)
 
     def product(i):
         return jnp.dot(lbuf[i], pbuf[i], preferred_element_type=F32)
 
-    group = 4 if blocks % 4 == 0 else 1
+    group = max(n for n in (1, 2, 4, 8, 16, 32) if blocks % n == 0)
 
     def left_products(arriving):
         acc[...] = jnp.zeros_like(acc)
@@ -426,7 +426,7 @@
             dma((ops,)),
         ],
         compiler_params=pltpu.CompilerParams(
-            collective_id=0, has_side_effects=True, vmem_limit_bytes=48 * 1024 * 1024
+            collective_id=0, has_side_effects=True, vmem_limit_bytes=60 * 1024 * 1024
         ),
     )(left_arrival, right, op_charge, sector_dims, wavefunction, onsite)
 

time: 159 us -> 152 us (0.956)
  local copies, waits for them, and re-layouts: 5.97 us -> 2.92 us
  Pallas kernels: 151 us -> 148 us
    pallas_call x1, Pallas kernels: 151 us -> 148 us  [on_device(): pl.pallas_call(functools.partial(davidson_kernel, sectors, ops), out_shap...]
    unnamed x10 -> x2, local copies, waits for them, and re-layouts: 5.97 us -> 2.92 us
where the time goes in v3:
time: 152 us
  Pallas kernels  148 us (97%)
  local copies, waits for them, and re-layouts  2.92 us (2%)
    pallas_call x1, Pallas kernels, on_device(): pl.pallas_call(functools.partial(davidson_kernel, sectors, ops), out_shap...  148 us

profile of v3, /device:TPU:1, one launch (start us, length us, event | category | flops | bytes accessed | tf_op | source)
XLA Modules:
  0.0 152.2 jit_solution(7608658859036306694)
XLA Ops:
  1.3 148.0 %shard_map.77 = (f32[1,256,256]{2,1,0:T(8,128)}, f32[3,3]{1,0:T(4,128)}) custom-call(bf16[8,4,256,256]{3,2,1,0:T(8,128)(2,1)} %left_ref.1, bf16[32,256,256]{2,1,0:T(8,128)(2,1)} %bitcast.1, s32[128]{0:T(128)} %charge_hbm.1, s32[1]{0:T(128)S(6)} %copy.10.dims_hbm, bf16[1,256,256]{2,1,0:T(8,128)(2,1)} %wave_hbm.1, f32[1,256,256]{2,1,0:T(8,128)} %onsite_hbm.1), custom_call_target="tpu_custom_call" | custom-call | tf_op jit(solution)/shard_map/pallas_call | solution.py:390
  149.3 1.7 %copy.11 = f32[1,256,256]{2,1,0:T(8,128)} copy(f32[1,256,256]{2,1,0:T(8,128)} %get-tuple-element.4) | data formatting | bytes 524288
  151.0 1.2 copy.12

commit v4 on v3

--- a/solution.py
+++ b/solution.py
@@ -168,6 +168,13 @@
             else:
                 pl.when((t + d >= 0) & (t + d < sectors))(run)
 
+    def each_op(action):
+        def step(p, carry):
+            action(lax.rem(q + p, ops))
+            return carry
+
+        lax.fori_loop(1, ops, step, 0, unroll=True)
+
     def send_vector(j, values):
         held[j][1, mine] = values
         each_reader(lambda d, o: vector_copy(j, d, o, q).start())
@@ -201,8 +208,42 @@
     lax.fori_loop(0, early, send_left, 0)
     start_norm = take_sums(0)[0]
     vector = (masked / jnp.sqrt(start_norm / entries + 1e-06)).astype(BF16)
-    send_vector(0, vector)
+    def relay_copy(d, o, source):
+        return pltpu.make_async_remote_copy(
+            src_ref=v0.at[d + 1, rows_of(source)],
+            dst_ref=v0.at[d + 1, rows_of(source)],
+            send_sem=v_send.at[0, d + 1, o],
+            recv_sem=v_recv.at[0, d + 1, source],
+            device_id=device(t, o),
+            device_id_type=MESH,
+        )
+
+    def present(d):
+        return (t + d >= 0) & (t + d < sectors)
+
+    v0[1, mine] = vector
+    for d in (1, -1):
+        @pl.when(present(d))
+        def _(d=d):
+            vector_copy(0, d, q, q).start()
+    each_op(lambda o: relay_copy(0, o, q).start())
     lax.fori_loop(early, remote_blocks, send_left, 0)
+    for d in (1, -1):
+        @pl.when(present(-d))
+        def _(d=d):
+            vector_copy(0, d, q, q).wait_recv()
+            each_op(lambda o: relay_copy(d, o, q).start())
+    each_op(lambda o: relay_copy(0, o, o).wait_recv())
+    for d in (1, -1):
+        @pl.when(present(-d))
+        def _(d=d):
+            each_op(lambda o: relay_copy(d, o, o).wait_recv())
+            each_op(lambda o: relay_copy(d, o, q).wait_send())
+
+        @pl.when(present(d))
+        def _(d=d):
+            vector_copy(0, d, q, q).wait_send()
+    each_op(lambda o: relay_copy(0, o, q).wait_send())
     right_copy.wait()
     own_copy.wait()
 
@@ -258,13 +299,6 @@
             device_id_type=MESH,
         )
 
-    def each_op(action):
-        def step(p, carry):
-            action(lax.rem(q + p, ops))
-            return carry
-
-        lax.fori_loop(1, ops, step, 0, unroll=True)
-
     def send_partial(j):
         part_send[j] = acc[...].astype(BF16)
         each_op(lambda o: part_copy(j, o, q).start())
@@ -285,7 +319,8 @@
     cross = []
     for j in range(3):
         current = vectors[j].astype(F32)
-        take_vector(j)
+        if j > 0:
+            take_vector(j)
         right_products(j)
         left_products(j == 0)
         send_partial(j)

time: 152 us -> 150 us (0.987)
  Pallas kernels: 148 us -> 146 us
    pallas_call x1, Pallas kernels: 148 us -> 146 us  [on_device(): pl.pallas_call(functools.partial(davidson_kernel, sectors, ops), out_shap...]
where the time goes in v4:
time: 150 us
  Pallas kernels  146 us (97%)
  local copies, waits for them, and re-layouts  2.92 us (2%)
    pallas_call x1, Pallas kernels, on_device(): pl.pallas_call(functools.partial(davidson_kernel, sectors, ops), out_shap...  146 us

profile of v4, /device:TPU:1, one launch (start us, length us, event | category | flops | bytes accessed | tf_op | source)
XLA Modules:
  0.0 150.1 jit_solution(17764015334427334601)
XLA Ops:
  1.3 145.9 %shard_map.77 = (f32[1,256,256]{2,1,0:T(8,128)}, f32[3,3]{1,0:T(4,128)}) custom-call(bf16[8,4,256,256]{3,2,1,0:T(8,128)(2,1)} %left_ref.1, bf16[32,256,256]{2,1,0:T(8,128)(2,1)} %bitcast.1, s32[128]{0:T(128)} %charge_hbm.1, s32[1]{0:T(128)S(6)} %copy.10.dims_hbm, bf16[1,256,256]{2,1,0:T(8,128)(2,1)} %wave_hbm.1, f32[1,256,256]{2,1,0:T(8,128)} %onsite_hbm.1), custom_call_target="tpu_custom_call" | custom-call | tf_op jit(solution)/shard_map/pallas_call | solution.py:425
  147.2 1.7 %copy.11 = f32[1,256,256]{2,1,0:T(8,128)} copy(f32[1,256,256]{2,1,0:T(8,128)} %get-tuple-element.4) | data formatting | bytes 524288
  148.9 1.2 copy.12

commit v5 on v4

--- a/solution.py
+++ b/solution.py
@@ -256,7 +256,7 @@
             ).astype(BF16)
             return carry
 
-        lax.fori_loop(0, blocks, step, 0, unroll=8)
+        lax.fori_loop(0, blocks, step, 0, unroll=16)
 
     def product(i):
         return jnp.dot(lbuf[i], pbuf[i], preferred_element_type=F32)

time: 150 us -> 149 us (level)
  no operation moved by 1% of the time
where the time goes in v5:
time: 149 us
  Pallas kernels  145 us (97%)
  local copies, waits for them, and re-layouts  2.92 us (2%)
    pallas_call x1, Pallas kernels, on_device(): pl.pallas_call(functools.partial(davidson_kernel, sectors, ops), out_shap...  145 us

profile of v5, /device:TPU:1, one launch (start us, length us, event | category | flops | bytes accessed | tf_op | source)
XLA Modules:
  0.0 149.3 jit_solution(14798021487164449725)
XLA Ops:
  1.3 145.1 %shard_map.77 = (f32[1,256,256]{2,1,0:T(8,128)}, f32[3,3]{1,0:T(4,128)}) custom-call(bf16[8,4,256,256]{3,2,1,0:T(8,128)(2,1)} %left_ref.1, bf16[32,256,256]{2,1,0:T(8,128)(2,1)} %bitcast.1, s32[128]{0:T(128)} %charge_hbm.1, s32[1]{0:T(128)S(6)} %copy.10.dims_hbm, bf16[1,256,256]{2,1,0:T(8,128)(2,1)} %wave_hbm.1, f32[1,256,256]{2,1,0:T(8,128)} %onsite_hbm.1), custom_call_target="tpu_custom_call" | custom-call | tf_op jit(solution)/shard_map/pallas_call | solution.py:425
  146.4 1.7 %copy.11 = f32[1,256,256]{2,1,0:T(8,128)} copy(f32[1,256,256]{2,1,0:T(8,128)} %get-tuple-element.4) | data formatting | bytes 524288
  148.1 1.2 copy.12
